TPU v7x, 256 devices: a whole 4x4x8 slice. The times are simulated.
256 devices in a mesh: expert: 16 (over z, core), fsdp: 16 (over x, y).
Axes of the slice: x: 4, y: 4, z: 8, core: 2. Of those that a mesh axis runs over, the one named last changes fastest.
Arguments:
- grad_blocks: bfloat16 [16, 16, 512, 512], P('expert', None, 'fsdp'), may hold values from -42 to 42
- second_moment: float32 [16, 16, 512, 512], P('expert', None, 'fsdp'), may hold values from 0.1 to 2
- block_order: int32 [16, 16], P('expert'), may hold values from 0 to 15, as said below
- left_stat: float32 [256, 512, 512], P(('expert', 'fsdp')), may hold values from -1 to 3, as said below
- right_stat: float32 [256, 512, 512], P(('expert', 'fsdp')), may hold values from -1 to 3, as said below
- left_root: bfloat16 [256, 512, 512], P(('expert', 'fsdp')), may hold values from -1 to 2, as said below
- right_root: bfloat16 [256, 512, 512], P(('expert', 'fsdp')), may hold values from -1 to 2, as said below
Outputs:
- direction: float32 [16, 16, 512, 512], P('expert', None, 'fsdp')
- second_new: float32 [16, 16, 512, 512], P('expert', None, 'fsdp')
- left_stat_new: float32 [256, 512, 512], P(('expert', 'fsdp'))
- right_stat_new: float32 [256, 512, 512], P(('expert', 'fsdp'))
- left_root_new: bfloat16 [256, 512, 512], P(('expert', 'fsdp'))
- right_root_new: bfloat16 [256, 512, 512], P(('expert', 'fsdp'))
Inputs may be any that keep to these rules, and one draw needn't show every extreme that they name: `block_order`: every row is a permutation of 0 to 15. `left_stat`: symmetric and positive definite. `right_stat`: symmetric and positive definite. `left_root`: symmetric. `right_root`: symmetric.
All inputs are finite; a program needn't handle non-finite values.
Results may differ from a plain program's by a relative error of at most 0.0049.
Values may be sent and summed in bfloat16 or wider, within the bound.
A program may use at most 64 MiB of HBM per device.

v0:
```python
import functools

import jax
import jax.numpy as jnp
from jax import lax
from jax.experimental import pallas as pl
from jax.experimental.pallas import tpu as pltpu
from jax.sharding import PartitionSpec as P

MESH = pl.DeviceIdType.MESH
N = 16
ROWS = 32
BLK = 512
F32 = jnp.float32
BF16 = jnp.bfloat16


def dot(a, b, dims=((1,), (0,))):
    return lax.dot_general(a, b, (dims, ((), ())), preferred_element_type=F32)


def split(x):
    high = x.astype(BF16)
    return high, (x - high.astype(F32)).astype(BF16)


def target(step, expert, turn):
    m = lax.rem(lax.rem(step, 8) + turn, 8)
    dz = jnp.where(lax.rem(m, 2) == 1, (m + 1) // 2, 8 - m // 2)
    return lax.rem(expert // 2 + dz, 8) * 2 + step // 8


def wait_bytes(ref, sem):
    pltpu.make_async_copy(ref, ref, sem).wait()


def exchange_kernel(
    order_hbm, grad_hbm, second_hbm, lstat_hbm, rstat_hbm, lroot_hbm, rroot_hbm,
    home, factor, second_new, stat_new, root_new,
    order, grad, second, stat, root, staged, block, shaped, passing, rows, part, parts, pow_hi, pow_lo,
    load_sem, scat_send, scat_recv, hop_send, hop_recv, home_send, home_recv, part_send, part_recv, here_sem, go_sem,
):
    e = lax.axis_index("expert")
    r = lax.axis_index("fsdp")
    diagonal = e == r

    barrier = pltpu.get_barrier_semaphore()

    @pl.loop(0, N)
    def _(i):
        @pl.when(jnp.logical_not(diagonal & (i == r)))
        def _():
            pl.semaphore_signal(barrier, inc=1, device_id=(r, i), device_id_type=MESH)

    loads = [
        pltpu.make_async_copy(grad_hbm, grad, load_sem.at[0]),
        pltpu.make_async_copy(second_hbm, second, load_sem.at[1]),
        pltpu.make_async_copy(lroot_hbm, root.at[0], load_sem.at[2]),
        pltpu.make_async_copy(rroot_hbm, root.at[1], load_sem.at[3]),
        pltpu.make_async_copy(lstat_hbm, stat.at[0], load_sem.at[4]),
        pltpu.make_async_copy(rstat_hbm, stat.at[1], load_sem.at[5]),
    ]
    load_order = pltpu.make_async_copy(order_hbm, order, load_sem.at[6])
    load_order.start()
    for load in loads:
        load.start()

    load_order.wait()
    loads[0].wait()

    @pl.loop(0, N)
    def _(i):
        staged[i] = grad[order[0, i]]

    pl.semaphore_wait(barrier, jnp.where(diagonal, N - 1, N))

    @pl.loop(0, N)
    def _(k):
        i = target(k, e, r)
        stays = diagonal & (i == e)

        @pl.when(jnp.logical_not(stays))
        def _():
            pltpu.make_async_remote_copy(
                staged.at[i], block.at[r], scat_send, scat_recv, device_id=(i, e), device_id_type=MESH
            ).start()

        @pl.when(stays)
        def _():
            pltpu.make_async_copy(staged.at[i], block.at[r], scat_recv).start()

    @pl.when(jnp.logical_not(diagonal))
    def _():
        pl.semaphore_signal(here_sem, inc=1, device_id=(e, e), device_id_type=MESH)

    loads[1].wait()

    @pl.loop(0, N)
    def _(j):
        value = grad[j].astype(F32)
        moment = 0.95 * second[j] + 0.05 * value * value
        second_new[j] = moment
        step = value / (jnp.sqrt(moment) + 1e-08)
        rows[pl.ds(j, 1), :] = jnp.sum(step * step, axis=0, keepdims=True)

    diag_mask = lax.broadcasted_iota(jnp.int32, (N, 128), 0) == lax.broadcasted_iota(jnp.int32, (N, 128), 1)
    sums = jnp.sum(rows[...], axis=1, keepdims=True)
    part[...] = jnp.sum(jnp.where(diag_mask, sums, 0.0), axis=0, keepdims=True)
    parts[r] = part[...]

    @pl.when(diagonal)
    def _():
        pl.semaphore_wait(here_sem, N - 1)

        @pl.loop(1, N)
        def _(k):
            pl.semaphore_signal(go_sem, inc=1, device_id=(e, lax.rem(r + k, N)), device_id_type=MESH)

    loads[2].wait()
    loads[3].wait()

    @pl.loop(0, 2)
    def _(side):
        x = root[side]
        square_hi, square_lo = split(dot(x, x))
        cube_hi, cube_lo = split(dot(x, square_hi) + dot(x, square_lo))
        fifth = dot(cube_hi, square_hi) + dot(cube_hi, square_lo) + dot(cube_lo, square_hi)
        high, low = split(fifth)
        pow_hi[side] = high
        pow_lo[side] = low

    @pl.when(jnp.logical_not(diagonal))
    def _():
        pl.semaphore_wait(go_sem, 1)

    @pl.loop(1, N)
    def _(k):
        pltpu.make_async_remote_copy(
            part, parts.at[r], part_send, part_recv, device_id=(e, lax.rem(r + k, N)), device_id_type=MESH
        ).start()

    wait_bytes(block, scat_recv)
    g = block[...].reshape(BLK, BLK)
    half = dot(root[0], g).astype(BF16)
    step = dot(half, root[1])
    norm = jnp.sum(jnp.sum(step * step, axis=0, keepdims=True), axis=1, keepdims=True)
    scale = 1.0 / jnp.sqrt(norm + 1e-06)
    shaped[...] = (step * scale).astype(BF16).reshape(N, ROWS, BLK)

    @pl.loop(0, N)
    def _(k):
        i = lax.rem(r + k + e, N)

        @pl.when(i != r)
        def _():
            pltpu.make_async_remote_copy(
                shaped.at[i], passing.at[k], hop_send, hop_recv.at[k], device_id=(e, i), device_id_type=MESH
            ).start()

        @pl.when(i == r)
        def _():
            pltpu.make_async_copy(shaped.at[i], passing.at[k], hop_recv.at[k]).start()

    loads[4].wait()
    stat_new[0] = 0.95 * stat[0] + (0.05 / BLK) * dot(g, g, ((1,), (1,)))

    @pl.loop(0, N)
    def _(k):
        f = lax.rem(r + 2 * N - k - e, N)
        wait_bytes(passing.at[k], hop_recv.at[k])

        @pl.when(f != e)
        def _():
            pltpu.make_async_remote_copy(
                passing.at[k], home.at[e], home_send, home_recv, device_id=(f, r), device_id_type=MESH
            ).start()

        @pl.when(f == e)
        def _():
            pltpu.make_async_copy(passing.at[k], home.at[e], home_recv).start()

    loads[5].wait()
    stat_new[1] = 0.95 * stat[1] + (0.05 / BLK) * dot(g, g, ((0,), (0,)))

    @pl.loop(0, 2)
    def _(side):
        stat_hi, stat_lo = split(stat_new[side])
        product = dot(pow_hi[side], stat_hi) + dot(pow_hi[side], stat_lo) + dot(pow_lo[side], stat_hi)
        root_new[side] = (0.25 * (5.0 * root[side].astype(F32) - product)).astype(BF16)

    wait_bytes(parts.at[pl.ds(0, N - 1)], part_recv)
    total = jnp.sum(parts[...], axis=0)
    column = jnp.sum(jnp.where(diag_mask, total, 0.0), axis=1, keepdims=True)
    factor[...] = jnp.broadcast_to(jnp.sqrt(column), (N, BLK))

    wait_bytes(parts.at[pl.ds(0, N - 1)], part_send)

    @pl.when(diagonal)
    def _():
        wait_bytes(staged.at[pl.ds(0, N - 1)], scat_send)

    @pl.when(jnp.logical_not(diagonal))
    def _():
        wait_bytes(staged, scat_send)

    wait_bytes(shaped.at[pl.ds(0, N - 1)], hop_send)
    wait_bytes(passing.at[pl.ds(0, N - 1)], home_send)
    wait_bytes(home, home_recv)


def finish_kernel(
    order, home, factor, second_new, stat_new, root_new,
    direction, second_out, lstat_out, rstat_out, lroot_out, rroot_out,
    wide, sems,
):
    copies = [
        pltpu.make_async_copy(second_new, second_out, sems.at[0]),
        pltpu.make_async_copy(stat_new.at[0], lstat_out, sems.at[1]),
        pltpu.make_async_copy(stat_new.at[1], rstat_out, sems.at[2]),
        pltpu.make_async_copy(root_new.at[0], lroot_out, sems.at[3]),
        pltpu.make_async_copy(root_new.at[1], rroot_out, sems.at[4]),
    ]
    for copy in copies:
        copy.start()

    @pl.loop(0, N)
    def _(i):
        j = order[i]
        wide[j] = home[i].astype(F32) * factor[pl.ds(j, 1), :]

    last = pltpu.make_async_copy(wide, direction, sems.at[5])
    last.start()
    for copy in copies:
        copy.wait()
    last.wait()


def local(grad_blocks, second_moment, block_order, left_stat, right_stat, left_root, right_root):
    order = block_order[0]
    any_spec = pl.BlockSpec(memory_space=pl.ANY)
    hbm_spec = pl.BlockSpec(memory_space=pltpu.HBM)
    vmem_spec = pl.BlockSpec(memory_space=pltpu.VMEM)
    smem_spec = pl.BlockSpec(memory_space=pltpu.SMEM)
    dma = pltpu.SemaphoreType.DMA
    piece = (N, ROWS, BLK)
    pair = (2, BLK, BLK)
    products = 2 * BLK**3
    results = pl.pallas_call(
        exchange_kernel,
        out_shape=[
            pltpu.VMEM(piece, BF16),
            pltpu.VMEM((N, BLK), F32),
            pltpu.VMEM(piece, F32),
            pltpu.VMEM(pair, F32),
            pltpu.VMEM(pair, BF16),
        ],
        in_specs=[hbm_spec] * 7,
        out_specs=[vmem_spec] * 5,
        scratch_shapes=[
            pltpu.SMEM((1, N), jnp.int32),
            pltpu.VMEM(piece, BF16),
            pltpu.VMEM(piece, F32),
            pltpu.VMEM(pair, F32),
            pltpu.VMEM(pair, BF16),
            pltpu.VMEM(piece, BF16),
            pltpu.VMEM(piece, BF16),
            pltpu.VMEM(piece, BF16),
            pltpu.VMEM(piece, BF16),
            pltpu.VMEM((N, BLK), F32),
            pltpu.VMEM((1, 128), F32),
            pltpu.VMEM((N, 1, 128), F32),
            pltpu.VMEM(pair, BF16),
            pltpu.VMEM(pair, BF16),
            dma((7,)),
            dma,
            dma,
            dma,
            dma((N,)),
            dma,
            dma,
            dma,
            dma,
            pltpu.SemaphoreType.REGULAR,
            pltpu.SemaphoreType.REGULAR,
        ],
        compiler_params=pltpu.CompilerParams(
            collective_id=0, has_side_effects=True, vmem_limit_bytes=32 * 1024 * 1024
        ),
        cost_estimate=pl.CostEstimate(flops=22 * products, bytes_accessed=10 * 2**20, transcendentals=2**19),
        name="exchange",
    )(
        pltpu.with_memory_space_constraint(block_order, pltpu.HBM),
        *(
            pltpu.with_memory_space_constraint(x[0], pltpu.HBM)
            for x in (grad_blocks, second_moment, left_stat, right_stat, left_root, right_root)
        ),
    )
    outs = pl.pallas_call(
        finish_kernel,
        out_shape=[
            jax.ShapeDtypeStruct(piece, F32),
            jax.ShapeDtypeStruct(piece, F32),
            jax.ShapeDtypeStruct((BLK, BLK), F32),
            jax.ShapeDtypeStruct((BLK, BLK), F32),
            jax.ShapeDtypeStruct((BLK, BLK), BF16),
            jax.ShapeDtypeStruct((BLK, BLK), BF16),
        ],
        in_specs=[smem_spec] + [vmem_spec] * 5,
        out_specs=[any_spec] * 6,
        scratch_shapes=[pltpu.VMEM(piece, F32), dma((6,))],
        compiler_params=pltpu.CompilerParams(vmem_limit_bytes=32 * 1024 * 1024),
        cost_estimate=pl.CostEstimate(flops=2**19, bytes_accessed=10 * 2**20, transcendentals=0),
        name="finish",
    )(order, *results)
    return tuple(out[None] for out in outs)


def solution(mesh):
    placed = (
        P("expert", None, "fsdp", None),
        P("expert", None, "fsdp", None),
        P("expert", None),
        P(("expert", "fsdp"), None, None),
        P(("expert", "fsdp"), None, None),
        P(("expert", "fsdp"), None, None),
        P(("expert", "fsdp"), None, None),
    )
    return jax.shard_map(
        local,
        mesh=mesh,
        in_specs=placed,
        out_specs=(
            P("expert", None, "fsdp", None),
            P("expert", None, "fsdp", None),
            P(("expert", "fsdp"), None, None),
            P(("expert", "fsdp"), None, None),
            P(("expert", "fsdp"), None, None),
            P(("expert", "fsdp"), None, None),
        ),
        check_vma=False,
    )
```

profile of v0, /device:TPU:1, one launch (start us, length us, event | category | flops | bytes accessed | tf_op | source)
XLA Modules:
  0.0 47.8 jit_solution(13972882382902975558)
XLA Ops:
  0.6 0.0 copy-start
  0.6 44.2 %exchange.1 = (bf16[16,32,512]{2,1,0:T(8,128)(2,1)S(1)}, f32[16,512]{1,0:T(8,128)S(1)}, f32[16,32,512]{2,1,0:T(8,128)S(1)}, f32[2,512,512]{2,1,0:T(8,128)S(1)}, bf16[2,512,512]{2,1,0:T(8,128)(2,1)S(1)}) custom-call(s32[1,16]{1,0:T(1,128)} %order_hbm.1, bf16[16,32,512]{2,1,0:T(8,128)(2,1)} %bitcast.21, f32[16,32,512]{2,1,0:T(8,128)} %bitcast.14, ...), custom_call_target="tpu_custom_call" | custom-call | flops 5905580032 | bytes 10485760 | tf_op jit(solution)/shard_map/exchange/pallas_call | solution.py:248
  44.9 0.0 copy-done
  44.9 2.9 %finish.1 = (f32[16,32,512]{2,1,0:T(8,128)}, f32[16,32,512]{2,1,0:T(8,128)}, f32[512,512]{1,0:T(8,128)}, f32[512,512]{1,0:T(8,128)}, bf16[512,512]{1,0:T(8,128)(2,1)}, /*index=5*/bf16[512,512]{1,0:T(8,128)(2,1)}) custom-call(s32[16]{0:T(128)S(1)} %bitcast.13, bf16[16,32,512]{2,1,0:T(8,128)(2,1)S(1)} %get-tuple-element.17.home, ...), custom_call_target="tpu_custom_call" | custom-call | flops 524288 | bytes 10485760 | tf_op jit(solution)/shard_map/finish/pallas_call | solution.py:298
Async XLA Ops:
  0.6 44.2 %copy-start = (s32[1,16]{1,0:T(1,128)S(1)}, s32[1,16]{1,0:T(1,128)}, u32[]{:S(2)}) copy-start(s32[1,16]{1,0:T(1,128)} %order_hbm.1) | copy-start | bytes 196
where the time goes:
time: 47.9 us; the launch traced here: 47.8 us
  Pallas kernels  47.2 us (99%)
  between operations  0.66 us (1%)
    pallas_call x1, Pallas kernels, local(): pl.pallas_call(exchange_kernel, out_shape=[pltpu.VMEM(piece, BF16), pltpu...  44.2 us
    pallas_call x1, Pallas kernels, local(): pl.pallas_call(finish_kernel, out_shape=[jax.ShapeDtypeStruct(piece, F32)...  2.94 us

commit v1 on v0

--- a/solution.py
+++ b/solution.py
@@ -24,9 +24,18 @@
     return high, (x - high.astype(F32)).astype(BF16)
 
 
+def pick(index, values):
+    result = values[-1]
+    for at, value in enumerate(values[:-1]):
+        result = jnp.where(index == at, value, result)
+    return result
+
+
 def target(step, expert, turn):
-    m = lax.rem(lax.rem(step, 8) + turn, 8)
-    dz = jnp.where(lax.rem(m, 2) == 1, (m + 1) // 2, 8 - m // 2)
+    m = lax.rem(step, 4) + turn
+    far = pick(lax.rem(m, 4), (4, 3, 5, 6))
+    near = pick(lax.rem(m, 4), (2, 1, 7, 0))
+    dz = jnp.where(lax.rem(step, 8) < 4, far, near)
     return lax.rem(expert // 2 + dz, 8) * 2 + step // 8
 
 
@@ -209,10 +218,12 @@
 
 
 def finish_kernel(
-    order, home, factor, second_new, stat_new, root_new,
+    order_hbm, home, factor, second_new, stat_new, root_new,
     direction, second_out, lstat_out, rstat_out, lroot_out, rroot_out,
-    wide, sems,
+    order, wide, sems,
 ):
+    load = pltpu.make_async_copy(order_hbm, order, sems.at[6])
+    load.start()
     copies = [
         pltpu.make_async_copy(second_new, second_out, sems.at[0]),
         pltpu.make_async_copy(stat_new.at[0], lstat_out, sems.at[1]),
@@ -223,9 +234,11 @@
     for copy in copies:
         copy.start()
 
+    load.wait()
+
     @pl.loop(0, N)
     def _(i):
-        j = order[i]
+        j = order[0, i]
         wide[j] = home[i].astype(F32) * factor[pl.ds(j, 1), :]
 
     last = pltpu.make_async_copy(wide, direction, sems.at[5])
@@ -236,11 +249,10 @@
 
 
 def local(grad_blocks, second_moment, block_order, left_stat, right_stat, left_root, right_root):
-    order = block_order[0]
+    order = pltpu.with_memory_space_constraint(block_order, pltpu.HBM)
     any_spec = pl.BlockSpec(memory_space=pl.ANY)
     hbm_spec = pl.BlockSpec(memory_space=pltpu.HBM)
     vmem_spec = pl.BlockSpec(memory_space=pltpu.VMEM)
-    smem_spec = pl.BlockSpec(memory_space=pltpu.SMEM)
     dma = pltpu.SemaphoreType.DMA
     piece = (N, ROWS, BLK)
     pair = (2, BLK, BLK)
@@ -289,7 +301,7 @@
         cost_estimate=pl.CostEstimate(flops=22 * products, bytes_accessed=10 * 2**20, transcendentals=2**19),
         name="exchange",
     )(
-        pltpu.with_memory_space_constraint(block_order, pltpu.HBM),
+        order,
         *(
             pltpu.with_memory_space_constraint(x[0], pltpu.HBM)
             for x in (grad_blocks, second_moment, left_stat, right_stat, left_root, right_root)
@@ -305,9 +317,9 @@
             jax.ShapeDtypeStruct((BLK, BLK), BF16),
             jax.ShapeDtypeStruct((BLK, BLK), BF16),
         ],
-        in_specs=[smem_spec] + [vmem_spec] * 5,
+        in_specs=[hbm_spec] + [vmem_spec] * 5,
         out_specs=[any_spec] * 6,
-        scratch_shapes=[pltpu.VMEM(piece, F32), dma((6,))],
+        scratch_shapes=[pltpu.SMEM((1, N), jnp.int32), pltpu.VMEM(piece, F32), dma((7,))],
         compiler_params=pltpu.CompilerParams(vmem_limit_bytes=32 * 1024 * 1024),
         cost_estimate=pl.CostEstimate(flops=2**19, bytes_accessed=10 * 2**20, transcendentals=0),
         name="finish",

time: 47.9 us -> 46.2 us (0.965)
  Pallas kernels: 47.2 us -> 45.5 us
    pallas_call x1, Pallas kernels: 44.2 us -> 43.1 us  [local(): pl.pallas_call(exchange_kernel, out_shape=[pltpu.VMEM(piece, BF16), pltpu...]
    pallas_call x1, Pallas kernels: 2.94 us -> 2.42 us  [local(): pl.pallas_call(finish_kernel, out_shape=[jax.ShapeDtypeStruct(piece, F32)...]
where the time goes in v1:
time: 46.2 us; the launch traced here: 46.1 us
  Pallas kernels  45.5 us (98%)
  between operations  0.64 us (1%)
    pallas_call x1, Pallas kernels, local(): pl.pallas_call(exchange_kernel, out_shape=[pltpu.VMEM(piece, BF16), pltpu...  43.1 us
    pallas_call x1, Pallas kernels, local(): pl.pallas_call(finish_kernel, out_shape=[jax.ShapeDtypeStruct(piece, F32)...  2.42 us

profile of v1, /device:TPU:1, one launch (start us, length us, event | category | flops | bytes accessed | tf_op | source)
XLA Modules:
  0.0 46.1 jit_solution(14671208910839219700)
XLA Ops:
  0.6 43.1 %exchange.1 = (bf16[16,32,512]{2,1,0:T(8,128)(2,1)S(1)}, f32[16,512]{1,0:T(8,128)S(1)}, f32[16,32,512]{2,1,0:T(8,128)S(1)}, f32[2,512,512]{2,1,0:T(8,128)S(1)}, bf16[2,512,512]{2,1,0:T(8,128)(2,1)S(1)}) custom-call(s32[1,16]{1,0:T(1,128)} %order_hbm.3, bf16[16,32,512]{2,1,0:T(8,128)(2,1)} %bitcast.19, f32[16,32,512]{2,1,0:T(8,128)} %bitcast.12, ...), custom_call_target="tpu_custom_call" | custom-call | flops 5905580032 | bytes 10485760 | tf_op jit(solution)/shard_map/exchange/pallas_call | solution.py:260
  43.7 2.4 %finish.1 = (f32[16,32,512]{2,1,0:T(8,128)}, f32[16,32,512]{2,1,0:T(8,128)}, f32[512,512]{1,0:T(8,128)}, f32[512,512]{1,0:T(8,128)}, bf16[512,512]{1,0:T(8,128)(2,1)}, /*index=5*/bf16[512,512]{1,0:T(8,128)(2,1)}) custom-call(s32[1,16]{1,0:T(1,128)} %order_hbm.3, bf16[16,32,512]{2,1,0:T(8,128)(2,1)S(1)} %get-tuple-element.17.home, ...), custom_call_target="tpu_custom_call" | custom-call | flops 524288 | bytes 10485760 | tf_op jit(solution)/shard_map/finish/pallas_call | solution.py:310

commit v2 on v1

--- a/solution.py
+++ b/solution.py
@@ -46,20 +46,12 @@
 def exchange_kernel(
     order_hbm, grad_hbm, second_hbm, lstat_hbm, rstat_hbm, lroot_hbm, rroot_hbm,
     home, factor, second_new, stat_new, root_new,
-    order, grad, second, stat, root, staged, block, shaped, passing, rows, part, parts, pow_hi, pow_lo,
+    order, grad, second, stat, root, staged, block, half, wide, shaped, passing, rows, part, parts, pow_hi, pow_lo,
     load_sem, scat_send, scat_recv, hop_send, hop_recv, home_send, home_recv, part_send, part_recv, here_sem, go_sem,
 ):
     e = lax.axis_index("expert")
     r = lax.axis_index("fsdp")
     diagonal = e == r
-
-    barrier = pltpu.get_barrier_semaphore()
-
-    @pl.loop(0, N)
-    def _(i):
-        @pl.when(jnp.logical_not(diagonal & (i == r)))
-        def _():
-            pl.semaphore_signal(barrier, inc=1, device_id=(r, i), device_id_type=MESH)
 
     loads = [
         pltpu.make_async_copy(grad_hbm, grad, load_sem.at[0]),
@@ -71,7 +63,17 @@
     ]
     load_order = pltpu.make_async_copy(order_hbm, order, load_sem.at[6])
     load_order.start()
-    for load in loads:
+    loads[0].start()
+
+    barrier = pltpu.get_barrier_semaphore()
+
+    @pl.loop(0, N)
+    def _(i):
+        @pl.when(jnp.logical_not(diagonal & (i == r)))
+        def _():
+            pl.semaphore_signal(barrier, inc=1, device_id=(r, i), device_id_type=MESH)
+
+    for load in loads[1:]:
         load.start()
 
     load_order.wait()
@@ -150,15 +152,22 @@
 
     wait_bytes(block, scat_recv)
     g = block[...].reshape(BLK, BLK)
-    half = dot(root[0], g).astype(BF16)
-    step = dot(half, root[1])
-    norm = jnp.sum(jnp.sum(step * step, axis=0, keepdims=True), axis=1, keepdims=True)
+    half[...] = dot(root[0], g).astype(BF16)
+    squares = jnp.zeros((8, BLK), F32)
+    for j in range(4):
+        step = dot(half[j * 128 : (j + 1) * 128, :], root[1])
+        wide[j * 128 : (j + 1) * 128, :] = step
+        squares = squares + jnp.sum((step * step).reshape(16, 8, BLK), axis=0)
+    norm = jnp.sum(jnp.sum(squares, axis=0, keepdims=True), axis=1, keepdims=True)
     scale = 1.0 / jnp.sqrt(norm + 1e-06)
-    shaped[...] = (step * scale).astype(BF16).reshape(N, ROWS, BLK)
+    for j in range(4):
+        step = (wide[j * 128 : (j + 1) * 128, :] * scale).astype(BF16)
+        shaped[j * 4 : (j + 1) * 4] = step.reshape(4, ROWS, BLK)
 
     @pl.loop(0, N)
     def _(k):
-        i = lax.rem(r + k + e, N)
+        q = lax.rem(lax.rem(r, 4) * 4 + r // 4 + k + e, N)
+        i = lax.rem(q, 4) * 4 + q // 4
 
         @pl.when(i != r)
         def _():
@@ -175,7 +184,8 @@
 
     @pl.loop(0, N)
     def _(k):
-        f = lax.rem(r + 2 * N - k - e, N)
+        q = lax.rem(lax.rem(r, 4) * 4 + r // 4 + 2 * N - k - e, N)
+        f = lax.rem(q, 4) * 4 + q // 4
         wait_bytes(passing.at[k], hop_recv.at[k])
 
         @pl.when(f != e)
@@ -240,12 +250,11 @@
     def _(i):
         j = order[0, i]
         wide[j] = home[i].astype(F32) * factor[pl.ds(j, 1), :]
-
-    last = pltpu.make_async_copy(wide, direction, sems.at[5])
-    last.start()
+        pltpu.make_async_copy(wide.at[j], direction.at[j], sems.at[5]).start()
+
     for copy in copies:
         copy.wait()
-    last.wait()
+    pltpu.make_async_copy(wide, direction, sems.at[5]).wait()
 
 
 def local(grad_blocks, second_moment, block_order, left_stat, right_stat, left_root, right_root):
@@ -276,6 +285,8 @@
             pltpu.VMEM(pair, BF16),
             pltpu.VMEM(piece, BF16),
             pltpu.VMEM(piece, BF16),
+            pltpu.VMEM((BLK, BLK), BF16),
+            pltpu.VMEM((BLK, BLK), F32),
             pltpu.VMEM(piece, BF16),
             pltpu.VMEM(piece, BF16),
             pltpu.VMEM((N, BLK), F32),

time: 46.2 us -> 45.3 us (0.981); the launches traced: 46.1 us -> 44.8 us
  Pallas kernels: 45.5 us -> 44.1 us
    pallas_call x1, Pallas kernels: 43.1 us -> 41.7 us  [local(): pl.pallas_call(exchange_kernel, out_shape=[pltpu.VMEM(piece, BF16), pltpu...]
where the time goes in v2:
time: 45.3 us; the launch traced here: 44.8 us
  Pallas kernels  44.1 us (97%)
  between operations  0.64 us (1%)
    pallas_call x1, Pallas kernels, local(): pl.pallas_call(exchange_kernel, out_shape=[pltpu.VMEM(piece, BF16), pltpu...  41.7 us
    pallas_call x1, Pallas kernels, local(): pl.pallas_call(finish_kernel, out_shape=[jax.ShapeDtypeStruct(piece, F32)...  2.37 us

profile of v2, /device:TPU:1, one launch (start us, length us, event | category | flops | bytes accessed | tf_op | source)
XLA Modules:
  0.0 44.8 jit_solution(11982042339291736210)
XLA Ops:
  0.6 41.7 %exchange.1 = (bf16[16,32,512]{2,1,0:T(8,128)(2,1)S(1)}, f32[16,512]{1,0:T(8,128)S(1)}, f32[16,32,512]{2,1,0:T(8,128)S(1)}, f32[2,512,512]{2,1,0:T(8,128)S(1)}, bf16[2,512,512]{2,1,0:T(8,128)(2,1)S(1)}) custom-call(s32[1,16]{1,0:T(1,128)} %order_hbm.3, bf16[16,32,512]{2,1,0:T(8,128)(2,1)} %bitcast.19, f32[16,32,512]{2,1,0:T(8,128)} %bitcast.12, ...), custom_call_target="tpu_custom_call" | custom-call | flops 5905580032 | bytes 10485760 | tf_op jit(solution)/shard_map/exchange/pallas_call | solution.py:269
  42.4 2.4 %finish.1 = (f32[16,32,512]{2,1,0:T(8,128)}, f32[16,32,512]{2,1,0:T(8,128)}, f32[512,512]{1,0:T(8,128)}, f32[512,512]{1,0:T(8,128)}, bf16[512,512]{1,0:T(8,128)(2,1)}, /*index=5*/bf16[512,512]{1,0:T(8,128)(2,1)}) custom-call(s32[1,16]{1,0:T(1,128)} %order_hbm.3, bf16[16,32,512]{2,1,0:T(8,128)(2,1)S(1)} %get-tuple-element.17.home, ...), custom_call_target="tpu_custom_call" | custom-call | flops 524288 | bytes 10485760 | tf_op jit(solution)/shard_map/finish/pallas_call | solution.py:321

commit v3 on v2

--- a/solution.py
+++ b/solution.py
@@ -52,6 +52,7 @@
     e = lax.axis_index("expert")
     r = lax.axis_index("fsdp")
     diagonal = e == r
+    turn = e // 2 * 2 + 8 * lax.rem(e, 2)
 
     loads = [
         pltpu.make_async_copy(grad_hbm, grad, load_sem.at[0]),
@@ -85,6 +86,10 @@
 
     pl.semaphore_wait(barrier, jnp.where(diagonal, N - 1, N))
 
+    @pl.when(jnp.logical_not(diagonal))
+    def _():
+        pl.semaphore_signal(here_sem, inc=1, device_id=(e, e), device_id_type=MESH)
+
     @pl.loop(0, N)
     def _(k):
         i = target(k, e, r)
@@ -100,9 +105,13 @@
         def _():
             pltpu.make_async_copy(staged.at[i], block.at[r], scat_recv).start()
 
-    @pl.when(jnp.logical_not(diagonal))
-    def _():
-        pl.semaphore_signal(here_sem, inc=1, device_id=(e, e), device_id_type=MESH)
+    @pl.when(diagonal)
+    def _():
+        pl.semaphore_wait(here_sem, N - 1)
+
+        @pl.loop(1, N)
+        def _(k):
+            pl.semaphore_signal(go_sem, inc=1, device_id=(e, lax.rem(r + k, N)), device_id_type=MESH)
 
     loads[1].wait()
 
@@ -118,14 +127,6 @@
     sums = jnp.sum(rows[...], axis=1, keepdims=True)
     part[...] = jnp.sum(jnp.where(diag_mask, sums, 0.0), axis=0, keepdims=True)
     parts[r] = part[...]
-
-    @pl.when(diagonal)
-    def _():
-        pl.semaphore_wait(here_sem, N - 1)
-
-        @pl.loop(1, N)
-        def _(k):
-            pl.semaphore_signal(go_sem, inc=1, device_id=(e, lax.rem(r + k, N)), device_id_type=MESH)
 
     loads[2].wait()
     loads[3].wait()
@@ -166,7 +167,7 @@
 
     @pl.loop(0, N)
     def _(k):
-        q = lax.rem(lax.rem(r, 4) * 4 + r // 4 + k + e, N)
+        q = lax.rem(lax.rem(r, 4) * 4 + r // 4 + k + turn, N)
         i = lax.rem(q, 4) * 4 + q // 4
 
         @pl.when(i != r)
@@ -184,7 +185,7 @@
 
     @pl.loop(0, N)
     def _(k):
-        q = lax.rem(lax.rem(r, 4) * 4 + r // 4 + 2 * N - k - e, N)
+        q = lax.rem(lax.rem(r, 4) * 4 + r // 4 + 3 * N - k - turn, N)
         f = lax.rem(q, 4) * 4 + q // 4
         wait_bytes(passing.at[k], hop_recv.at[k])
 

time: 45.3 us -> 44.9 us (level); the launches traced: 44.8 us -> 44.8 us
  no operation moved by 1% of the time
where the time goes in v3:
time: 44.9 us; the launch traced here: 44.8 us
  Pallas kernels  44.2 us (98%)
  between operations  0.64 us (1%)
    pallas_call x1, Pallas kernels, local(): pl.pallas_call(exchange_kernel, out_shape=[pltpu.VMEM(piece, BF16), pltpu...  41.8 us
    pallas_call x1, Pallas kernels, local(): pl.pallas_call(finish_kernel, out_shape=[jax.ShapeDtypeStruct(piece, F32)...  2.37 us

profile of v3, /device:TPU:1, one launch (start us, length us, event | category | flops | bytes accessed | tf_op | source)
XLA Modules:
  0.0 44.8 jit_solution(15014620844836329342)
XLA Ops:
  0.6 41.8 %exchange.1 = (bf16[16,32,512]{2,1,0:T(8,128)(2,1)S(1)}, f32[16,512]{1,0:T(8,128)S(1)}, f32[16,32,512]{2,1,0:T(8,128)S(1)}, f32[2,512,512]{2,1,0:T(8,128)S(1)}, bf16[2,512,512]{2,1,0:T(8,128)(2,1)S(1)}) custom-call(s32[1,16]{1,0:T(1,128)} %order_hbm.3, bf16[16,32,512]{2,1,0:T(8,128)(2,1)} %bitcast.19, f32[16,32,512]{2,1,0:T(8,128)} %bitcast.12, ...), custom_call_target="tpu_custom_call" | custom-call | flops 5905580032 | bytes 10485760 | tf_op jit(solution)/shard_map/exchange/pallas_call | solution.py:270
  42.4 2.4 %finish.1 = (f32[16,32,512]{2,1,0:T(8,128)}, f32[16,32,512]{2,1,0:T(8,128)}, f32[512,512]{1,0:T(8,128)}, f32[512,512]{1,0:T(8,128)}, bf16[512,512]{1,0:T(8,128)(2,1)}, /*index=5*/bf16[512,512]{1,0:T(8,128)(2,1)}) custom-call(s32[1,16]{1,0:T(1,128)} %order_hbm.3, bf16[16,32,512]{2,1,0:T(8,128)(2,1)S(1)} %get-tuple-element.17.home, ...), custom_call_target="tpu_custom_call" | custom-call | flops 524288 | bytes 10485760 | tf_op jit(solution)/shard_map/finish/pallas_call | solution.py:322
